TPU v7x, 512 devices: a whole 4x8x8 slice. The times are simulated.
512 devices in a mesh: seq: 64 (over y, z), mp: 8 (over x, core).
Axes of the slice: x: 4, y: 8, z: 8, core: 2. Of those that a mesh axis runs over, the one named last changes fastest.
Arguments:
- inputs: bfloat16 [40960, 6144], P('seq', 'mp'), may hold values from -6 to 6
- queries: bfloat16 [40960, 4096], P('seq', 'mp'), may hold values from -12 to 12
- key_rows: bfloat16 [40960, 4096], P('seq', 'mp'), may hold values from -12 to 12
- values: bfloat16 [40960, 4096], P('seq', 'mp'), may hold values from -6 to 6
- norm_gain: float32 [4096], P('mp'), may hold values from 0.1 to 1.9
- cotangent: bfloat16 [40960, 4096], P('seq', 'mp'), may hold values from -6 to 6
- adapter_down: float32 [32, 6144], P(None, 'mp'), may hold values from -6 to 6
- adapter_up: float32 [32, 4096], P(None, 'mp'), may hold values from -6 to 6
- moment_down: float32 [32, 6144], P(None, 'mp'), may hold values from -6 to 6
- moment_up: float32 [32, 4096], P(None, 'mp'), may hold values from -6 to 6
- noise_down: float32 [32, 6144], P(None, 'mp'), may hold values from -6 to 6
- noise_up: float32 [32, 4096], P(None, 'mp'), may hold values from -6 to 6
Outputs:
- normed: bfloat16 [40960, 4096], P('seq', 'mp')
- new_down: float32 [32, 6144], P(None, 'mp')
- new_moment_down: float32 [32, 6144], P(None, 'mp')
- new_up: float32 [32, 4096], P(None, 'mp')
- new_moment_up: float32 [32, 4096], P(None, 'mp')
All inputs are finite; a program needn't handle non-finite values.
Results may differ from a plain program's by a relative error of at most 0.007.
Values sent between devices are 32-bit elements; how exact they have to be, the bound alone decides.
A program may use at most 128 MiB of HBM per device.

v0:
```python
import math
import jax
import jax.numpy as jnp
from jax import lax
from jax.sharding import PartitionSpec as P

D = 6144
HEAD = 128
RANK = 32
STEP = 250
CYCLE = 1000
friction = 0.2
peak_rate = 0.03
epsilon = 1e-06


def carried_in(x, axis, combine, identity, reverse):
    size, mine = (lax.axis_size(axis), lax.axis_index(axis))
    everything = lax.all_gather(x, axis)
    start = jnp.broadcast_to(jnp.asarray(identity, x.dtype), x.shape)

    def step(k, before):
        at = size - 1 - k if reverse else k
        reached = at > mine if reverse else at < mine
        new = combine(before, everything[at])
        return jnp.where(reached, new, before)

    return lax.fori_loop(0, size, step, start)


def combine_states(earlier, later_part):
    return earlier + later_part


def feature_map(array):
    return (jax.nn.elu(array.astype(jnp.float32)) + 1.0).astype(jnp.bfloat16)


def sghmc_step(parameter, moment, gradient, noise_term):
    step_rate = peak_rate * (math.cos(math.pi * ((STEP - 1) % CYCLE) / CYCLE) + 1.0)
    spread = math.sqrt(2.0 * friction * step_rate)
    moment_new = (1.0 - friction) * moment - step_rate * gradient + spread * noise_term
    return (parameter + moment_new, moment_new)


def per_device(
    inputs,
    queries,
    key_rows,
    values,
    norm_gain,
    cotangent,
    adapter_down,
    adapter_up,
    moment_down,
    moment_up,
    noise_down,
    noise_up,
):
    token_count = queries.shape[0]
    column_count = queries.shape[1]
    heads_here = column_count // HEAD
    blocked = (token_count, heads_here, HEAD)
    down_half = adapter_down.astype(jnp.bfloat16)
    up_half = adapter_up.astype(jnp.bfloat16)
    partial_inner = lax.dot_general(
        down_half, inputs, (((1,), (1,)), ((), ())), preferred_element_type=jnp.float32
    )
    inner_sum = lax.psum(partial_inner, "mp") / math.sqrt(D)
    inner_half = inner_sum.astype(jnp.bfloat16)
    lifted = lax.dot_general(
        inner_half, up_half, (((0,), (0,)), ((), ())), preferred_element_type=jnp.float32
    )
    value_mix = (
        (values.astype(jnp.float32) + lifted / math.sqrt(RANK))
        .astype(jnp.bfloat16)
        .reshape(blocked)
    )
    query_feat = feature_map(queries).reshape(blocked)
    key_feat = feature_map(key_rows).reshape(blocked)
    own_states = jnp.einsum("thd,the->hde", key_feat, value_mix, preferred_element_type=jnp.float32)
    prefix = carried_in(own_states, "seq", combine_states, jnp.zeros_like(own_states), False)
    positions = jnp.arange(token_count, dtype=jnp.int32)
    causal = positions[:, None] >= positions[None, :]
    scores = jnp.einsum("thd,shd->hts", query_feat, key_feat, preferred_element_type=jnp.float32)
    weights = jnp.where(causal[None], scores, 0.0).astype(jnp.bfloat16)
    nearby = jnp.einsum("hts,she->the", weights, value_mix, preferred_element_type=jnp.float32)
    carried = jnp.einsum(
        "thd,hde->the", query_feat, prefix.astype(jnp.bfloat16), preferred_element_type=jnp.float32
    )
    summed = nearby + carried
    gain_rows = norm_gain.reshape(heads_here, HEAD)
    inverse_norm = lax.rsqrt(jnp.mean(summed * summed, axis=-1, keepdims=True) + epsilon)
    unit_rows = summed * inverse_norm
    normed = (gain_rows * unit_rows).astype(jnp.bfloat16).reshape(token_count, column_count)
    gain_grad = gain_rows * cotangent.astype(jnp.float32).reshape(blocked)
    projected = jnp.mean(gain_grad * unit_rows, axis=-1, keepdims=True)
    out_grad = (inverse_norm * (gain_grad - unit_rows * projected)).astype(jnp.bfloat16)
    back_states = jnp.einsum(
        "thd,the->hde", query_feat, out_grad, preferred_element_type=jnp.float32
    )
    suffix = carried_in(back_states, "seq", combine_states, jnp.zeros_like(back_states), True)
    grad_near = jnp.einsum("hts,the->she", weights, out_grad, preferred_element_type=jnp.float32)
    grad_far = jnp.einsum(
        "shd,hde->she", key_feat, suffix.astype(jnp.bfloat16), preferred_element_type=jnp.float32
    )
    grad_half = (grad_near + grad_far).astype(jnp.bfloat16).reshape(token_count, column_count)
    partial_grad = lax.dot_general(
        up_half, grad_half, (((1,), (1,)), ((), ())), preferred_element_type=jnp.float32
    )
    inner_grad = lax.psum(partial_grad, "mp") / math.sqrt(RANK)
    inner_grad_half = inner_grad.astype(jnp.bfloat16)
    grad_down = jnp.dot(inner_grad_half, inputs, preferred_element_type=jnp.float32) / math.sqrt(D)
    grad_up = jnp.dot(inner_half, grad_half, preferred_element_type=jnp.float32) / math.sqrt(RANK)
    down_total, up_total = lax.psum((grad_down, grad_up), "seq")
    new_down, new_moment_down = sghmc_step(adapter_down, moment_down, down_total, noise_down)
    new_up, new_moment_up = sghmc_step(adapter_up, moment_up, up_total, noise_up)
    return (normed, new_down, new_moment_down, new_up, new_moment_up)


def solution(mesh):
    return jax.shard_map(
        per_device,
        mesh=mesh,
        in_specs=(
            P("seq", "mp"),
            P("seq", "mp"),
            P("seq", "mp"),
            P("seq", "mp"),
            P("mp"),
            P("seq", "mp"),
            P(None, "mp"),
            P(None, "mp"),
            P(None, "mp"),
            P(None, "mp"),
            P(None, "mp"),
            P(None, "mp"),
        ),
        out_specs=(P("seq", "mp"), P(None, "mp"), P(None, "mp"), P(None, "mp"), P(None, "mp")),
        check_vma=False,
    )
```

profile of v0, /device:TPU:2, one launch (start us, length us, event | category | flops | bytes accessed | tf_op | source)
XLA Modules:
  0.0 741.7 jit_solution(5236267360927953539)
XLA Ops:
  7.2 1.1 copy-done
  8.4 1.9 fusion.21
  10.7 69.7 %all-reduce.5.cloned.1.call-done = f32[32,640]{1,0:T(8,128)} async-done(((f32[32,640]{1,0:T(8,128)}), f32[32,640]{1,0:T(8,128)}) %all-reduce.5.cloned.1.call-update) | async-done | bytes 81936 | tf_op jit(solution)/shard_map/psum | solution.py:69
  80.4 1.3 fusion.2
  82.6 1.5 fusion.11
  85.0 1.6 copy.37
  86.8 2.9 select_convert_fusion
  89.6 1.7 copy-done.1
  91.3 2.2 fusion.30
  93.5 132.1 %all-gather.5.cloned.1.call-done = f32[256,128,128]{2,1,0:T(8,128)} async-done(((f32[4,128,128]{2,1,0:T(8,128)}), f32[256,128,128]{2,1,0:T(8,128)}) %all-gather.5.cloned.1.call-update) | async-done | bytes 16777232 | tf_op jit(solution)/shard_map/all_gather | solution.py:19
  225.6 68.1 %while.30 = (s32[]{:T(128)}, f32[4,128,128]{2,1,0:T(8,128)S(1)}, s32[]{:T(128)}, f32[64,4,128,128]{3,2,1,0:T(8,128)}, s32[]{:T(128)}, /*index=5*/s32[]{:T(128)}) while((s32[]{:T(128)}, f32[4,128,128]{2,1,0:T(8,128)S(1)}, s32[]{:T(128)}, f32[64,4,128,128]{3,2,1,0:T(8,128)}, s32[]{:T(128)}, /*index=5*/s32[]{:T(128)}) %tuple.95), condition=%wide.region_2.3_spmd.clone, body=%wide.region_1.2_spmd.clone.sunk | while | flops 196612 | bytes 786533 | solution.py:28
  227.7 1.0 add_select_fusion.4
  229.8 1.0 add_select_fusion.4
  232.0 1.0 add_select_fusion.4
  234.1 1.0 add_select_fusion.4
  236.2 1.0 add_select_fusion.4
  238.4 1.0 add_select_fusion.4
  247.9 1.0 add_select_fusion.4
  250.1 1.0 add_select_fusion.4
  252.2 1.0 add_select_fusion.4
  254.3 1.0 add_select_fusion.4
  256.4 1.0 add_select_fusion.4
  258.6 1.0 add_select_fusion.4
  268.2 1.0 add_select_fusion.4
  270.3 1.0 add_select_fusion.4
  272.4 1.0 add_select_fusion.4
  274.5 1.0 add_select_fusion.4
  276.7 1.0 add_select_fusion.4
  278.8 1.0 add_select_fusion.4
  288.4 1.0 add_select_fusion.4
  290.5 1.0 add_select_fusion.4
  292.6 1.0 add_select_fusion.4
  293.7 1.7 multiply_reduce_fusion.1
  295.8 1.2 multiply_convert_fusion
  297.0 1.1 fusion.32
  298.2 3.8 fusion.31
  302.0 134.4 %all-gather.7.cloned.1.call-done = f32[256,128,128]{2,1,0:T(8,128)} async-done(((f32[4,128,128]{2,1,0:T(8,128)}), f32[256,128,128]{2,1,0:T(8,128)}) %all-gather.7.cloned.1.call-update) | async-done | bytes 16777232 | tf_op jit(solution)/shard_map/all_gather | solution.py:19
  436.4 68.5 %while.31 = (s32[]{:T(128)}, f32[4,128,128]{2,1,0:T(8,128)S(1)}, s32[]{:T(128)}, f32[64,4,128,128]{3,2,1,0:T(8,128)}, s32[]{:T(128)}, /*index=5*/s32[]{:T(128)}, s32[]{:T(128)}, s32[]{:T(128)}) while((s32[]{:T(128)}, f32[4,128,128]{2,1,0:T(8,128)S(1)}, s32[]{:T(128)}, f32[64,4,128,128]{3,2,1,0:T(8,128)}, s32[]{:T(128)}, ...), condition=%wide.region_6.7_spmd.clone, body=%wide.region_5.6_spmd.clone.sunk | while | flops 196616 | bytes 786595 | solution.py:28
  436.4 1.1 add_select_fusion.5
  438.6 1.0 add_select_fusion.5
  504.9 2.1 fusion.3
  507.0 1.1 convolution_bitcast_fusion
  509.1 66.0 %all-reduce.7.cloned.1.call-done = f32[32,640]{0,1:T(8,128)} async-done(((f32[32,640]{0,1:T(8,128)}), f32[32,640]{0,1:T(8,128)}) %all-reduce.7.cloned.1.call-update) | async-done | bytes 81936 | tf_op jit(solution)/shard_map/psum | solution.py:111
  575.1 1.9 convolution_multiply_fusion.1
  577.1 1.1 copy.42
  578.2 153.8 %all-reduce.9.cloned.1.call-done = (f32[32,768]{1,0:T(8,128)}, f32[32,512]{1,0:T(8,128)}) async-done(((f32[32,768]{1,0:T(8,128)}, f32[32,512]{1,0:T(8,128)}), (f32[32,768]{1,0:T(8,128)}, f32[32,512]{1,0:T(8,128)})) %all-reduce.9.cloned.1.call-update) | async-done | bytes 163856 | tf_op jit(solution)/shard_map/psum | solution.py:115
  732.0 1.6 fusion.29
  733.6 1.5 fusion.28
  (161 shorter events, 113.0 us)
Async XLA Ops:
  7.2 1.2 copy-start
  7.2 3.2 copy-start.7
  7.2 73.3 %copy-start.9 = (f32[32,512]{1,0:T(8,128)S(1)}, f32[32,512]{1,0:T(8,128)}, u32[]{:S(2)}) copy-start(f32[32,512]{1,0:T(8,128)} %param.23) | copy-start | bytes 196612
  7.2 73.2 %all-reduce.5.cloned.1.call-start = ((), (), s32[]{:S(2)}) async-start(), calls=%async_computation | async-start | bytes 163840 | tf_op jit(solution)/shard_map/psum | solution.py:69
  10.3 72.2 %copy-start.17 = (bf16[640,512]{1,0:T(8,128)(2,1)S(1)}, bf16[640,512]{1,0:T(8,128)(2,1)}, u32[]{:S(2)}) copy-start(bf16[640,512]{1,0:T(8,128)(2,1)} %param.18) | copy-start | bytes 1966084
  10.4 215.2 %all-gather.5.cloned.1.call-start = ((), (), s32[]{:S(2)}) async-start(), calls=%async_computation.2 | async-start | bytes 17039360 | tf_op jit(solution)/shard_map/all_gather | solution.py:19
  81.7 0.8 copy-start.4
  82.5 1.6 copy-start.8
  84.1 352.3 %all-gather.7.cloned.1.call-start = ((), (), s32[]{:S(2)}) async-start(), calls=%async_computation.3 | async-start | bytes 17039360 | tf_op jit(solution)/shard_map/all_gather | solution.py:19
  85.0 208.6 %copy-start.2 = (bf16[640,512]{0,1:T(8,128)(2,1)}, bf16[640,512]{0,1:T(8,128)(2,1)S(1)}, u32[]{:S(2)}) copy-start(bf16[640,512]{0,1:T(8,128)(2,1)S(1)} %copy.47) | copy-start | bytes 1966084
  86.8 4.6 copy-start.5
  89.6 1.7 copy-start.1
  293.7 1.8 copy-start.16
  295.8 1.2 copy-start.3
  298.1 277.0 %all-reduce.7.cloned.1.call-start = ((), (), s32[]{:S(2)}) async-start(), calls=%async_computation.1 | async-start | bytes 655360 | tf_op jit(solution)/shard_map/psum | solution.py:111
  436.4 68.5 %copy-start.18 = (bf16[640,512]{1,0:T(8,128)(2,1)S(1)}, bf16[640,512]{1,0:T(8,128)(2,1)}, u32[]{:S(2)}) copy-start(bf16[640,512]{1,0:T(8,128)(2,1)} %param.18) | copy-start | bytes 1966084
  507.0 1.2 copy-start.11
  508.1 69.0 %copy-start.6 = (bf16[640,4,128]{0,2,1:T(8,128)(2,1)S(1)}, bf16[640,4,128]{0,2,1:T(8,128)(2,1)}, u32[]{:S(2)}) copy-start(bf16[640,4,128]{0,2,1:T(8,128)(2,1)} %get-tuple-element.259) | copy-start | bytes 1966084
  508.1 223.9 %all-reduce.9.cloned.1.call-start = ((), (), s32[]{:S(2)}) async-start(), calls=%async_computation.4 | async-start | bytes 327680 | tf_op jit(solution)/shard_map/psum | solution.py:115
  509.1 222.9 %copy-start.10 = (f32[32,768]{1,0:T(8,128)S(1)}, f32[32,768]{1,0:T(8,128)}, u32[]{:S(2)}) copy-start(f32[32,768]{1,0:T(8,128)} %param.22) | copy-start | bytes 294916
  509.1 222.9 %copy-start.12 = (f32[32,768]{1,0:T(8,128)S(1)}, f32[32,768]{1,0:T(8,128)}, u32[]{:S(2)}) copy-start(f32[32,768]{1,0:T(8,128)} %param.26) | copy-start | bytes 294916
  509.1 222.9 %copy-start.13 = (f32[32,768]{1,0:T(8,128)S(1)}, f32[32,768]{1,0:T(8,128)}, u32[]{:S(2)}) copy-start(f32[32,768]{1,0:T(8,128)} %param.24) | copy-start | bytes 294916
  577.1 156.6 %copy-start.14 = (f32[32,512]{1,0:T(8,128)S(1)}, f32[32,512]{1,0:T(8,128)}, u32[]{:S(2)}) copy-start(f32[32,512]{1,0:T(8,128)} %param.27) | copy-start | bytes 196612
  577.1 156.6 %copy-start.15 = (f32[32,512]{1,0:T(8,128)S(1)}, f32[32,512]{1,0:T(8,128)}, u32[]{:S(2)}) copy-start(f32[32,512]{1,0:T(8,128)} %param.25) | copy-start | bytes 196612
Sparse Core Ops, SparseCore 0:
  10.9 69.4 all-reduce.4
  84.2 141.3 all-gather.4
  298.3 138.1 all-gather.6
  508.3 66.8 all-reduce.6
  579.0 153.0 all-reduce.8
where the time goes:
time: 746 us; the launch traced here: 742 us
  waiting for transfers between devices  556 us (75%)
  other arithmetic  139 us (19%)
  matrix products  22.4 us (3%)
  between operations  14 us (2%)
    all_gather x2, waiting for transfers between devices, carried_in(): everything = lax.all_gather(x, axis)  267 us
    psum x1, waiting for transfers between devices, per_device(): down_total, up_total = lax.psum((grad_down, grad_up), 'seq')  154 us
    select_n x128, other arithmetic, step(): return jnp.where(reached, new, before)  133 us
    psum x1, waiting for transfers between devices, per_device(): inner_sum = lax.psum(partial_inner, 'mp') / math.sqrt(D)  69.7 us
    psum x1, waiting for transfers between devices, per_device(): inner_grad = lax.psum(partial_grad, 'mp') / math.sqrt(RANK)  66 us
  transfers between devices with their start and end apart: 5, of which 5 were waited for; matrix products, arithmetic and copies ran while one was open for 2% of the time, Pallas kernels for 0%

commit v1 on v0

--- a/solution.py
+++ b/solution.py
@@ -66,7 +66,7 @@
     partial_inner = lax.dot_general(
         down_half, inputs, (((1,), (1,)), ((), ())), preferred_element_type=jnp.float32
     )
-    inner_sum = lax.psum(partial_inner, "mp") / math.sqrt(D)
+    inner_sum = jnp.sum(lax.all_gather(partial_inner, "mp"), axis=0) / math.sqrt(D)
     inner_half = inner_sum.astype(jnp.bfloat16)
     lifted = lax.dot_general(
         inner_half, up_half, (((0,), (0,)), ((), ())), preferred_element_type=jnp.float32

time: 746 us -> 692 us (0.928)
  waiting for transfers between devices: 556 us -> 487 us
  blocking collectives: 0 us -> 16.5 us
    psum x1 -> x0, waiting for transfers between devices: 69.7 us -> none  [per_device(): inner_sum = lax.psum(partial_inner, 'mp') / math.sqrt(D)]
    all_gather x0 -> x1, blocking collectives: none -> 16.5 us  [per_device(): lax.all_gather(partial_inner, 'mp')]
  transfers between devices with their start and end apart: 5 -> 4, of which waited for: 5 -> 4; matrix products, arithmetic and copies ran while one was open for 2% -> 2% of each run, Pallas kernels for 0% -> 0%
where the time goes in v1:
time: 692 us; the launch traced here: 687 us
  waiting for transfers between devices  487 us (70%)
  other arithmetic  139 us (20%)
  matrix products  20.9 us (3%)
  blocking collectives  16.5 us (2%)
  between operations  14 us (2%)
  local copies, waits for them, and re-layouts  6.95 us (1%)
    all_gather x2, waiting for transfers between devices, carried_in(): everything = lax.all_gather(x, axis)  266 us
    psum x1, waiting for transfers between devices, per_device(): down_total, up_total = lax.psum((grad_down, grad_up), 'seq')  154 us
    select_n x128, other arithmetic, step(): return jnp.where(reached, new, before)  133 us
    psum x1, waiting for transfers between devices, per_device(): inner_grad = lax.psum(partial_grad, 'mp') / math.sqrt(RANK)  66 us
    all_gather x1, blocking collectives, per_device(): lax.all_gather(partial_inner, 'mp')  16.5 us
  transfers between devices with their start and end apart: 4, of which 4 were waited for; matrix products, arithmetic and copies ran while one was open for 2% of the time, Pallas kernels for 0%

profile of v1, /device:TPU:2, one launch (start us, length us, event | category | flops | bytes accessed | tf_op | source)
XLA Modules:
  0.0 687.2 jit_solution(15470054727030804714)
XLA Ops:
  7.2 1.1 copy-done
  8.4 1.3 fusion.21
  9.7 16.5 %all-gather = f32[256,640]{1,0:T(8,128)S(1)} all-gather(f32[32,640]{1,0:T(8,128)S(1)} %fusion.21), channel_id=2, replica_groups=mesh['seq'=64,'mp'=8] {'mp'}, dimensions={0}, use_global_device_ids=true | all-gather | bytes 737280 | tf_op jit(solution)/shard_map/all_gather | solution.py:69
  27.7 1.5 fusion.11
  30.2 1.6 copy.37
  31.9 2.9 select_convert_fusion
  34.8 1.7 copy-done.1
  36.5 2.2 fusion.30
  38.7 132.1 %all-gather.6.cloned.1.call-done = f32[256,128,128]{2,1,0:T(8,128)} async-done(((f32[4,128,128]{2,1,0:T(8,128)}), f32[256,128,128]{2,1,0:T(8,128)}) %all-gather.6.cloned.1.call-update) | async-done | bytes 16777232 | tf_op jit(solution)/shard_map/all_gather | solution.py:19
  170.7 68.1 %while.30 = (s32[]{:T(128)}, f32[4,128,128]{2,1,0:T(8,128)S(1)}, s32[]{:T(128)}, f32[64,4,128,128]{3,2,1,0:T(8,128)}, s32[]{:T(128)}, /*index=5*/s32[]{:T(128)}) while((s32[]{:T(128)}, f32[4,128,128]{2,1,0:T(8,128)S(1)}, s32[]{:T(128)}, f32[64,4,128,128]{3,2,1,0:T(8,128)}, s32[]{:T(128)}, /*index=5*/s32[]{:T(128)}) %tuple.93), condition=%wide.region_2.3_spmd.clone, body=%wide.region_1.2_spmd.clone.sunk | while | flops 196612 | bytes 786533 | solution.py:28
  238.8 1.7 multiply_reduce_fusion.1
  240.9 1.2 multiply_convert_fusion
  242.2 1.1 fusion.32
  243.3 3.8 fusion.31
  247.1 134.4 %all-gather.8.cloned.1.call-done = f32[256,128,128]{2,1,0:T(8,128)} async-done(((f32[4,128,128]{2,1,0:T(8,128)}), f32[256,128,128]{2,1,0:T(8,128)}) %all-gather.8.cloned.1.call-update) | async-done | bytes 16777232 | tf_op jit(solution)/shard_map/all_gather | solution.py:19
  381.5 68.5 %while.31 = (s32[]{:T(128)}, f32[4,128,128]{2,1,0:T(8,128)S(1)}, s32[]{:T(128)}, f32[64,4,128,128]{3,2,1,0:T(8,128)}, s32[]{:T(128)}, /*index=5*/s32[]{:T(128)}, s32[]{:T(128)}, s32[]{:T(128)}) while((s32[]{:T(128)}, f32[4,128,128]{2,1,0:T(8,128)S(1)}, s32[]{:T(128)}, f32[64,4,128,128]{3,2,1,0:T(8,128)}, s32[]{:T(128)}, ...), condition=%wide.region_6.7_spmd.clone, body=%wide.region_5.6_spmd.clone.sunk | while | flops 196616 | bytes 786595 | solution.py:28
  381.5 1.1 add_select_fusion.5
  383.7 1.0 add_select_fusion.5
  384.8 1.0 add_select_fusion.5
  387.0 1.0 add_select_fusion.5
  388.0 1.0 add_select_fusion.5
  390.2 1.0 add_select_fusion.5
  391.2 1.0 add_select_fusion.5
  393.4 1.0 add_select_fusion.5
  394.4 1.0 add_select_fusion.5
  397.7 1.0 add_select_fusion.5
  398.7 1.0 add_select_fusion.5
  400.9 1.0 add_select_fusion.5
  401.9 1.0 add_select_fusion.5
  404.1 1.0 add_select_fusion.5
  405.1 1.0 add_select_fusion.5
  407.3 1.0 add_select_fusion.5
  408.3 1.0 add_select_fusion.5
  410.5 1.0 add_select_fusion.5
  411.6 1.0 add_select_fusion.5
  413.7 1.0 add_select_fusion.5
  414.8 1.0 add_select_fusion.5
  418.0 1.0 add_select_fusion.5
  419.0 1.0 add_select_fusion.5
  421.2 1.0 add_select_fusion.5
  450.0 2.1 fusion.3
  452.2 1.1 convolution_bitcast_fusion
  454.3 66.0 %all-reduce.4.cloned.1.call-done = f32[32,640]{0,1:T(8,128)} async-done(((f32[32,640]{0,1:T(8,128)}), f32[32,640]{0,1:T(8,128)}) %all-reduce.4.cloned.1.call-update) | async-done | bytes 81936 | tf_op jit(solution)/shard_map/psum | solution.py:111
  520.3 1.9 convolution_multiply_fusion.1
  522.3 1.1 copy.42
  523.4 154.2 %all-reduce.6.cloned.1.call-done = (f32[32,768]{1,0:T(8,128)}, f32[32,512]{1,0:T(8,128)}) async-done(((f32[32,768]{1,0:T(8,128)}, f32[32,512]{1,0:T(8,128)}), (f32[32,768]{1,0:T(8,128)}, f32[32,512]{1,0:T(8,128)})) %all-reduce.6.cloned.1.call-update) | async-done | bytes 163856 | tf_op jit(solution)/shard_map/psum | solution.py:115
  677.6 1.6 fusion.29
  679.2 1.5 fusion.28
  (158 shorter events, 112.3 us)
Async XLA Ops:
  7.2 1.2 copy-start
  7.2 19.0 %copy-start.7 = (bf16[640,512]{1,0:T(8,128)(2,1)S(1)}, bf16[640,512]{1,0:T(8,128)(2,1)}, u32[]{:S(2)}) copy-start(bf16[640,512]{1,0:T(8,128)(2,1)} %param.19) | copy-start | bytes 1966084
  7.2 163.5 %all-gather.6.cloned.1.call-start = ((), (), s32[]{:S(2)}) async-start(), calls=%async_computation.1 | async-start | bytes 17039360 | tf_op jit(solution)/shard_map/all_gather | solution.py:19
  9.7 16.8 %copy-start.9 = (f32[32,512]{1,0:T(8,128)S(1)}, f32[32,512]{1,0:T(8,128)}, u32[]{:S(2)}) copy-start(f32[32,512]{1,0:T(8,128)} %param.23) | copy-start | bytes 196612
  26.5 1.2 copy-start.16
  26.9 0.8 copy-start.4
  27.7 1.6 copy-start.8
  29.2 352.3 %all-gather.8.cloned.1.call-start = ((), (), s32[]{:S(2)}) async-start(), calls=%async_computation.2 | async-start | bytes 17039360 | tf_op jit(solution)/shard_map/all_gather | solution.py:19
  30.2 208.6 %copy-start.2 = (bf16[640,512]{0,1:T(8,128)(2,1)}, bf16[640,512]{0,1:T(8,128)(2,1)S(1)}, u32[]{:S(2)}) copy-start(bf16[640,512]{0,1:T(8,128)(2,1)S(1)} %copy.47) | copy-start | bytes 1966084
  31.9 4.6 copy-start.5
  34.8 1.7 copy-start.1
  238.8 1.8 copy-start.15
  240.9 1.2 copy-start.3
  243.3 277.0 %all-reduce.4.cloned.1.call-start = ((), (), s32[]{:S(2)}) async-start(), calls=%async_computation | async-start | bytes 655360 | tf_op jit(solution)/shard_map/psum | solution.py:111
  381.5 68.5 %copy-start.17 = (bf16[640,512]{1,0:T(8,128)(2,1)S(1)}, bf16[640,512]{1,0:T(8,128)(2,1)}, u32[]{:S(2)}) copy-start(bf16[640,512]{1,0:T(8,128)(2,1)} %param.18) | copy-start | bytes 1966084
  453.3 69.0 %copy-start.6 = (bf16[640,4,128]{0,2,1:T(8,128)(2,1)S(1)}, bf16[640,4,128]{0,2,1:T(8,128)(2,1)}, u32[]{:S(2)}) copy-start(bf16[640,4,128]{0,2,1:T(8,128)(2,1)} %get-tuple-element.259) | copy-start | bytes 1966084
  453.3 224.2 %all-reduce.6.cloned.1.call-start = ((), (), s32[]{:S(2)}) async-start(), calls=%async_computation.3 | async-start | bytes 327680 | tf_op jit(solution)/shard_map/psum | solution.py:115
  454.3 223.3 %copy-start.10 = (f32[32,768]{1,0:T(8,128)S(1)}, f32[32,768]{1,0:T(8,128)}, u32[]{:S(2)}) copy-start(f32[32,768]{1,0:T(8,128)} %param.22) | copy-start | bytes 294916
  454.3 223.3 %copy-start.11 = (f32[32,768]{1,0:T(8,128)S(1)}, f32[32,768]{1,0:T(8,128)}, u32[]{:S(2)}) copy-start(f32[32,768]{1,0:T(8,128)} %param.26) | copy-start | bytes 294916
  454.3 223.3 %copy-start.12 = (f32[32,768]{1,0:T(8,128)S(1)}, f32[32,768]{1,0:T(8,128)}, u32[]{:S(2)}) copy-start(f32[32,768]{1,0:T(8,128)} %param.24) | copy-start | bytes 294916
  522.2 156.9 %copy-start.13 = (f32[32,512]{1,0:T(8,128)S(1)}, f32[32,512]{1,0:T(8,128)}, u32[]{:S(2)}) copy-start(f32[32,512]{1,0:T(8,128)} %param.27) | copy-start | bytes 196612
  522.2 156.9 %copy-start.14 = (f32[32,512]{1,0:T(8,128)S(1)}, f32[32,512]{1,0:T(8,128)}, u32[]{:S(2)}) copy-start(f32[32,512]{1,0:T(8,128)} %param.25) | copy-start | bytes 196612
Sparse Core Ops, SparseCore 0:
  29.4 141.2 all-gather.5
  243.4 138.1 all-gather.7
  453.4 66.8 all-reduce.3
  524.5 153.0 all-reduce.5
